TPU v7x, 32 devices: a whole 2x2x4 slice. The times are simulated.
32 devices in a mesh: leaf: 4 (over x, core), oct: 8 (over z, y).
Axes of the slice: x: 2, y: 2, z: 4, core: 2. Of those that a mesh axis runs over, the one named last changes fastest.
Arguments:
- dens_fine: bfloat16 [152, 4608], P(None, ('leaf', 'oct')), may hold values from -6 to 6
- parent: int32 [4608], P(('leaf', 'oct')), may hold values from 0 to 1023, as said below
- child_code: int32 [4608], P(('leaf', 'oct')), may hold values from 0 to 7, as said below
- m2m_ops: bfloat16 [152, 8, 152], replicated, may hold values from -0.15625 to 0.15625
- m2l_ops: bfloat16 [152, 152, 316], replicated, may hold values from -0.02734375 to 0.02734375
- ask_fine: int32 [32, 32, 16], P(('leaf', 'oct')), may hold values from -1 to 143, as said below
- list_fine: int32 [4608, 316], P(('leaf', 'oct')), may hold values from -1 to 655, as said below
- ask_coarse: int32 [32, 32, 8], P(('leaf', 'oct')), may hold values from -1 to 31, as said below
- list_coarse: int32 [1024, 316], P(('leaf', 'oct')), may hold values from -1 to 287, as said below
Outputs:
- pot_fine: float32 [152, 4608], P(None, ('leaf', 'oct'))
- pot_coarse: float32 [152, 1024], P(None, ('leaf', 'oct'))
Inputs may be any that keep to these rules, and one draw needn't show every extreme that they name: parent[i] is a coarse octant of the device that holds fine octant i; parents never fall along the array; every coarse octant has 1 to 8 children and some has 8. `child_code`: the children of one coarse octant carry distinct codes, increasing along the array. ask_fine[d, e] lists distinct fine octants of device e, then -1 to the end; row d, d is all -1; some row holds 16 octants. `list_fine`: an entry other than -1 names an own octant (below 144) or a slot of ask_fine[d] that isn't -1; each target has at most 189 entries other than -1, and some target has exactly 189. ask_coarse[d, e] lists distinct coarse octants of device e, then -1 to the end; row d, d is all -1; some row holds 8 octants. `list_coarse`: an entry other than -1 names an own octant (below 32) or a slot of ask_coarse[d] that isn't -1; each target has at most 189 entries other than -1, and some target has exactly 189.
All inputs are finite; a program needn't handle non-finite values.
Results may differ from a plain program's by a relative error of at most 0.0029.
Values may be sent and summed in bfloat16 or wider, within the bound.
No kernel may reach another device: no remote copies, remote signals or barrier semaphores. Data moves between devices by JAX's collectives and lax.ppermute only.
A program may use at most 192 MiB of HBM per device.

v0:
```python
import jax
import jax.numpy as jnp
from jax import lax
from jax.sharding import PartitionSpec as P


def with_blank(pieces, surface):
    return jnp.concatenate(list(pieces) + [jnp.zeros((1, surface), jnp.bfloat16)], axis=0)


def replies(dens_rows, wanted):
    own_count, surface = dens_rows.shape
    padded = with_blank([dens_rows], surface)
    chosen_rows = jnp.where(wanted < 0, own_count, wanted).reshape(-1)
    return padded[chosen_rows]


def translate(source_rows, entries, m2l_ops):
    surface = source_rows.shape[1]
    offsets = entries.shape[1]
    block_len = (offsets + 3) // 4
    accumulated = jnp.zeros((surface, entries.shape[0]), jnp.float32)
    for first_off in range(0, offsets, block_len):
        last_off = min(first_off + block_len, offsets)
        gathered = source_rows[entries[:, first_off:last_off]]
        accumulated = accumulated + jnp.einsum(
            "tcb,abc->at",
            gathered,
            m2l_ops[:, :, first_off:last_off],
            preferred_element_type=jnp.float32,
        )
    return accumulated


def body(
    dens_fine, parent, child_code, m2m_ops, m2l_ops, ask_fine, list_fine, ask_coarse, list_coarse
):
    surface, fine_own = dens_fine.shape
    coarse_own = list_coarse.shape[0]
    asks_fine = ask_fine.reshape(ask_fine.shape[1], ask_fine.shape[2])
    asks_coarse = ask_coarse.reshape(ask_coarse.shape[1], ask_coarse.shape[2])
    wanted_fine, wanted_coarse = (
        lax.all_to_all(asks_fine, ("leaf", "oct"), split_axis=0, concat_axis=0, tiled=True),
        lax.all_to_all(asks_coarse, ("leaf", "oct"), split_axis=0, concat_axis=0, tiled=True),
    )
    fine_rows = dens_fine.T
    outgoing = replies(fine_rows, wanted_fine)
    arrived = lax.all_to_all(outgoing, ("leaf", "oct"), split_axis=0, concat_axis=0, tiled=True)
    table_fine = with_blank([fine_rows, arrived], surface)
    blank_fine = table_fine.shape[0] - 1
    pot_fine = translate(table_fine, jnp.where(list_fine < 0, blank_fine, list_fine), m2l_ops)
    positions = jnp.arange(8, dtype=jnp.int32)
    spread = jnp.where(
        (child_code[None, :] == positions[:, None])[:, None, :],
        dens_fine[None],
        jnp.zeros((), jnp.bfloat16),
    )
    child_terms = jnp.dot(
        m2m_ops.reshape(surface, 8 * surface),
        spread.reshape(8 * surface, fine_own),
        preferred_element_type=jnp.float32,
    )
    my_index = lax.axis_index(("leaf", "oct"))
    local_parent = parent - my_index * coarse_own
    members = (local_parent[:, None] == jnp.arange(coarse_own, dtype=jnp.int32)[None, :]).astype(
        jnp.float32
    )
    dens_coarse = jnp.dot(child_terms, members, precision=lax.Precision.HIGHEST).astype(
        jnp.bfloat16
    )
    coarse_rows = dens_coarse.T
    reached = lax.all_to_all(
        replies(coarse_rows, wanted_coarse),
        ("leaf", "oct"),
        split_axis=0,
        concat_axis=0,
        tiled=True,
    )
    table_coarse = with_blank([coarse_rows, reached], surface)
    blank_row = table_coarse.shape[0] - 1
    source_rows = jnp.where(list_coarse < 0, blank_row, list_coarse)
    pot_coarse = 0.5 * translate(table_coarse, source_rows, m2l_ops)
    return (pot_fine, pot_coarse)


def solution(mesh):
    return jax.shard_map(
        body,
        mesh=mesh,
        in_specs=(
            P(None, ("leaf", "oct")),
            P(("leaf", "oct")),
            P(("leaf", "oct")),
            P(),
            P(),
            P(("leaf", "oct"), None, None),
            P(("leaf", "oct"), None),
            P(("leaf", "oct"), None, None),
            P(("leaf", "oct"), None),
        ),
        out_specs=(P(None, ("leaf", "oct")), P(None, ("leaf", "oct"))),
        check_vma=False,
    )
```

profile of v0, /device:TPU:8, one launch (start us, length us, event | category | flops | bytes accessed | tf_op | source)
XLA Modules:
  0.0 355.7 jit_solution(8707638670728226275)
XLA Ops:
  2.1 6.0 %all-to-all-start.2 = ((s32[32,1,8]{2,1,0:T(1,128)}), s32[32,1,8]{2,1,0:T(1,128)S(1)}, u32[]{:S(2)}, u32[]{:S(2)}) async-start(s32[32,1,8]{2,1,0:T(1,128)} %bitcast.11), calls=%async_computation.2 | async-start | bytes 32768 | tf_op jit(solution)/shard_map/all_to_all | solution.py:44
  9.9 22.2 %fusion.74 = (bf16[152,152,79]{2,1,0:T(8,128)(2,1)}, bf16[152,152,79]{2,1,0:T(8,128)(2,1)}, bf16[152,152,79]{2,1,0:T(8,128)(2,1)}, bf16[152,152,79]{2,1,0:T(8,128)(2,1)}) fusion(bf16[152,152,316]{2,1,0:T(8,128)(2,1)} %param.13), kind=kLoop, calls=%fused_computation.81 | loop fusion | bytes 29203456 | tf_op jit(solution)/shard_map/slice | solution.py:29
  35.0 5.8 %all-to-all-start = ((s32[32,1,16]{2,1,0:T(1,128)}), s32[32,1,16]{2,1,0:T(1,128)S(1)}, u32[]{:S(2)}, u32[]{:S(2)}) async-start(s32[32,1,16]{2,1,0:T(1,128)} %bitcast.1), calls=%async_computation | async-start | bytes 32768 | tf_op jit(solution)/shard_map/all_to_all | solution.py:43
  44.0 2.7 all-to-all-done
  46.7 3.7 %all-to-all-start.3 = ((bf16[32,8,152]{2,1,0:T(8,128)(2,1)}), bf16[32,8,152]{2,1,0:T(8,128)(2,1)S(1)}, u32[]{:S(2)}, u32[]{:S(2)}) async-start(bf16[32,8,152]{2,1,0:T(8,128)(2,1)} %bitcast.13), calls=%async_computation.3 | async-start | bytes 262144 | tf_op jit(solution)/shard_map/all_to_all | solution.py:72
  53.8 3.7 %all-to-all-done.3 = bf16[32,8,152]{2,1,0:T(8,128)(2,1)S(1)} async-done(((bf16[32,8,152]{2,1,0:T(8,128)(2,1)}), bf16[32,8,152]{2,1,0:T(8,128)(2,1)S(1)}, u32[]{:S(2)}, u32[]{:S(2)}) %all-to-all-start.3) | async-done | bytes 77856 | tf_op jit(solution)/shard_map/all_to_all | solution.py:72
  57.5 3.5 all-to-all-start.1
  61.1 7.8 %gather_fusion.6 = bf16[2528,152]{1,0:T(8,128)(2,1)S(1)} fusion(bf16[289,152]{1,0:T(8,128)(2,1)S(1)} %pad_maximum_fusion.1, s32[3072]{0:T(1024)S(1)} %pad_clamp_fusion.7), kind=kCustom, calls=%fused_computation.6 | custom fusion | bytes 1547136 | tf_op jit(solution)/shard_map/gather | solution.py:25
  69.8 5.4 %reshape.146 = bf16[32,79,152]{1,0,2:T(8,128)(2,1)} reshape(bf16[2528,152]{0,1:T(8,128)(2,1)S(1)} %copy.50) | data formatting | bytes 1537024 | tf_op jit(solution)/shard_map/gather | solution.py:25
  75.2 7.8 %gather_fusion.7 = bf16[2528,152]{1,0:T(8,128)(2,1)S(1)} fusion(bf16[289,152]{1,0:T(8,128)(2,1)S(1)} %pad_maximum_fusion.1, s32[3072]{0:T(1024)S(1)} %pad_clamp_fusion.6), kind=kCustom, calls=%fused_computation.7 | custom fusion | bytes 1547136 | tf_op jit(solution)/shard_map/gather | solution.py:25
  83.9 5.4 %reshape.154 = bf16[32,79,152]{1,0,2:T(8,128)(2,1)} reshape(bf16[2528,152]{0,1:T(8,128)(2,1)S(1)} %copy.51) | data formatting | bytes 1537024 | tf_op jit(solution)/shard_map/gather | solution.py:25
  89.3 7.8 %gather_fusion.8 = bf16[2528,152]{1,0:T(8,128)(2,1)S(1)} fusion(bf16[289,152]{1,0:T(8,128)(2,1)S(1)} %pad_maximum_fusion.1, s32[3072]{0:T(1024)S(1)} %pad_clamp_fusion.5), kind=kCustom, calls=%fused_computation.8 | custom fusion | bytes 1547136 | tf_op jit(solution)/shard_map/gather | solution.py:25
  98.0 5.3 %reshape.162 = bf16[32,79,152]{1,0,2:T(8,128)(2,1)} reshape(bf16[2528,152]{0,1:T(8,128)(2,1)S(1)} %copy.52) | data formatting | bytes 1537024 | tf_op jit(solution)/shard_map/gather | solution.py:25
  103.4 7.8 %gather_fusion.9 = bf16[2528,152]{1,0:T(8,128)(2,1)S(1)} fusion(bf16[289,152]{1,0:T(8,128)(2,1)S(1)} %pad_maximum_fusion.1, s32[3072]{0:T(1024)S(1)} %pad_clamp_fusion.4), kind=kCustom, calls=%fused_computation.9 | custom fusion | bytes 1547136 | tf_op jit(solution)/shard_map/gather | solution.py:25
  112.3 5.3 %reshape.170 = bf16[32,79,152]{1,0,2:T(8,128)(2,1)} reshape(bf16[2528,152]{0,1:T(8,128)(2,1)S(1)} %copy.53) | data formatting | bytes 1537024 | tf_op jit(solution)/shard_map/gather | solution.py:25
  117.6 5.2 %fusion.40 = f32[32,152]{1,0:T(8,128)S(1)} fusion(bf16[32,79,152]{1,0,2:T(8,128)(2,1)} %reshape.146, bf16[152,152,79]{2,1,0:T(8,128)(2,1)} %get-tuple-element.5), kind=kOutput, calls=%fused_computation.35 | convolution fusion | flops 116813824 | bytes 4438400 | tf_op jit(solution)/shard_map/tcb,abc->at/dot_general | solution.py:26
  122.8 4.8 %fusion.64 = f32[32,152]{1,0:T(8,128)S(1)} fusion(f32[32,152]{1,0:T(8,128)S(1)} %fusion.40, bf16[32,79,152]{1,0,2:T(8,128)(2,1)S(1)} %copy-done.2, bf16[152,152,79]{2,1,0:T(8,128)(2,1)} %get-tuple-element.4), kind=kOutput, calls=%fused_computation.43 | convolution fusion | flops 116818688 | bytes 4457856 | tf_op jit(solution)/shard_map/tcb,abc->at/dot_general | solution.py:26
  132.4 32.6 %gather_fusion.1 = bf16[11376,152]{1,0:T(8,128)(2,1)} fusion(bf16[657,152]{1,0:T(8,128)(2,1)S(1)} %pad_maximum_fusion, s32[12288]{0:T(1024)S(1)} %pad_clamp_fusion.3), kind=kCustom, calls=%fused_computation.1 | custom fusion | bytes 6962112 | tf_op jit(solution)/shard_map/gather | solution.py:25
  165.0 6.7 %copy.40 = bf16[11376,152]{0,1:T(8,128)(2,1)} copy(bf16[11376,152]{1,0:T(8,128)(2,1)} %gather_fusion.1) | data formatting | bytes 6916608 | tf_op jit(solution)/shard_map/gather | solution.py:25
  171.6 11.4 %reshape.106 = bf16[144,79,152]{1,0,2:T(8,128)(2,1)} reshape(bf16[11376,152]{0,1:T(8,128)(2,1)} %copy.40) | data formatting | bytes 6916608 | tf_op jit(solution)/shard_map/gather | solution.py:25
  183.1 6.0 %fusion.16 = f32[144,152]{1,0:T(8,128)S(1)} fusion(bf16[144,79,152]{1,0,2:T(8,128)(2,1)} %reshape.106, bf16[152,152,79]{2,1,0:T(8,128)(2,1)} %get-tuple-element.5), kind=kOutput, calls=%fused_computation.27 | convolution fusion | flops 525662208 | bytes 7196288 | tf_op jit(solution)/shard_map/tcb,abc->at/dot_general | solution.py:26
  189.1 32.6 %gather_fusion.2 = bf16[11376,152]{1,0:T(8,128)(2,1)} fusion(bf16[657,152]{1,0:T(8,128)(2,1)S(1)} %pad_maximum_fusion, s32[12288]{0:T(1024)S(1)} %pad_clamp_fusion.2), kind=kCustom, calls=%fused_computation.2 | custom fusion | bytes 6962112 | tf_op jit(solution)/shard_map/gather | solution.py:25
  221.7 6.9 %copy.42 = bf16[11376,152]{0,1:T(8,128)(2,1)} copy(bf16[11376,152]{1,0:T(8,128)(2,1)} %gather_fusion.2) | data formatting | bytes 6916608 | tf_op jit(solution)/shard_map/gather | solution.py:25
  228.6 11.4 %reshape.114 = bf16[144,79,152]{1,0,2:T(8,128)(2,1)} reshape(bf16[11376,152]{0,1:T(8,128)(2,1)} %copy.42) | data formatting | bytes 6916608 | tf_op jit(solution)/shard_map/gather | solution.py:25
  240.0 32.6 %gather_fusion.3 = bf16[11376,152]{1,0:T(8,128)(2,1)} fusion(bf16[657,152]{1,0:T(8,128)(2,1)S(1)} %pad_maximum_fusion, s32[12288]{0:T(1024)S(1)} %pad_clamp_fusion.1), kind=kCustom, calls=%fused_computation.3 | custom fusion | bytes 6962112 | tf_op jit(solution)/shard_map/gather | solution.py:25
  272.6 6.7 %copy.44 = bf16[11376,152]{0,1:T(8,128)(2,1)} copy(bf16[11376,152]{1,0:T(8,128)(2,1)} %gather_fusion.3) | data formatting | bytes 6916608 | tf_op jit(solution)/shard_map/gather | solution.py:25
  279.3 11.4 %reshape.122 = bf16[144,79,152]{1,0,2:T(8,128)(2,1)} reshape(bf16[11376,152]{0,1:T(8,128)(2,1)} %copy.44) | data formatting | bytes 6916608 | tf_op jit(solution)/shard_map/gather | solution.py:25
  290.7 32.6 %gather_fusion.4 = bf16[11376,152]{1,0:T(8,128)(2,1)} fusion(bf16[657,152]{1,0:T(8,128)(2,1)S(1)} %pad_maximum_fusion, s32[12288]{0:T(1024)S(1)} %pad_clamp_fusion), kind=kCustom, calls=%fused_computation.4 | custom fusion | bytes 6962112 | tf_op jit(solution)/shard_map/gather | solution.py:25
  323.3 6.7 %copy.46 = bf16[11376,152]{0,1:T(8,128)(2,1)} copy(bf16[11376,152]{1,0:T(8,128)(2,1)} %gather_fusion.4) | data formatting | bytes 6916608 | tf_op jit(solution)/shard_map/gather | solution.py:25
  330.0 11.5 %reshape.130 = bf16[144,79,152]{1,0,2:T(8,128)(2,1)} reshape(bf16[11376,152]{0,1:T(8,128)(2,1)} %copy.46) | data formatting | bytes 6916608 | tf_op jit(solution)/shard_map/gather | solution.py:25
  341.6 6.2 %fusion.37 = f32[144,152]{1,0:T(8,128)S(1)} fusion(f32[144,152]{1,0:T(8,128)S(1)} %fusion.16, bf16[144,79,152]{1,0,2:T(8,128)(2,1)} %reshape.114, bf16[152,152,79]{2,1,0:T(8,128)(2,1)} %get-tuple-element.4), kind=kOutput, calls=%fused_computation.34 | convolution fusion | flops 525684096 | bytes 7283840 | tf_op jit(solution)/shard_map/tcb,abc->at/dot_general | solution.py:26
  347.8 5.1 %fusion.34 = f32[144,152]{1,0:T(8,128)S(1)} fusion(f32[144,152]{1,0:T(8,128)S(1)} %fusion.37, bf16[144,79,152]{1,0,2:T(8,128)(2,1)} %reshape.122, bf16[152,152,79]{2,1,0:T(8,128)(2,1)S(1)} %bitcast.81), kind=kOutput, calls=%fused_computation.33 | convolution fusion | flops 525684096 | bytes 7283840 | tf_op jit(solution)/shard_map/tcb,abc->at/dot_general | solution.py:26
  (94 shorter events, 23.0 us)
Async XLA Ops:
  0.6 32.9 %copy-start = (bf16[152,8,152]{2,1,0:T(8,128)(2,1)S(1)}, bf16[152,8,152]{2,1,0:T(8,128)(2,1)}, u32[]{:S(2)}) copy-start(bf16[152,8,152]{2,1,0:T(8,128)(2,1)} %param.12) | copy-start | bytes 1108996
  2.1 33.0 %all-to-all-start.2 = ((s32[32,1,8]{2,1,0:T(1,128)}), s32[32,1,8]{2,1,0:T(1,128)S(1)}, u32[]{:S(2)}, u32[]{:S(2)}) async-start(s32[32,1,8]{2,1,0:T(1,128)} %bitcast.11), calls=%async_computation.2 | async-start | bytes 32768 | tf_op jit(solution)/shard_map/all_to_all | solution.py:44
  9.8 22.6 %copy-start.6 = (s32[144,316]{1,0:T(8,128)S(1)}, s32[144,316]{1,0:T(8,128)}, u32[]{:S(2)}) copy-start(s32[144,316]{1,0:T(8,128)} %param.15) | copy-start | bytes 546052
  9.8 23.7 %copy-start.8 = (s32[144]{0:T(256)S(1)}, s32[144]{0:T(256)}, u32[]{:S(2)}) copy-start(s32[144]{0:T(256)} %param.10) | copy-start | bytes 1732
  9.9 23.7 %copy-start.5 = (bf16[152,144]{0,1:T(8,128)(2,1)S(1)}, bf16[152,144]{0,1:T(8,128)(2,1)}, u32[]{:S(2)}) copy-start(bf16[152,144]{0,1:T(8,128)(2,1)} %param.9) | copy-start | bytes 131332
  9.9 24.5 %copy-start.7 = (s32[1,32,16]{1,2,0:T(8,128)S(1)}, s32[1,32,16]{1,2,0:T(8,128)}, u32[]{:S(2)}) copy-start(s32[1,32,16]{1,2,0:T(8,128)} %param.14) | copy-start | bytes 6148
  35.0 11.6 %all-to-all-start = ((s32[32,1,16]{2,1,0:T(1,128)}), s32[32,1,16]{2,1,0:T(1,128)S(1)}, u32[]{:S(2)}, u32[]{:S(2)}) async-start(s32[32,1,16]{2,1,0:T(1,128)} %bitcast.1), calls=%async_computation | async-start | bytes 32768 | tf_op jit(solution)/shard_map/all_to_all | solution.py:43
  46.7 10.8 %all-to-all-start.3 = ((bf16[32,8,152]{2,1,0:T(8,128)(2,1)}), bf16[32,8,152]{2,1,0:T(8,128)(2,1)S(1)}, u32[]{:S(2)}, u32[]{:S(2)}) async-start(bf16[32,8,152]{2,1,0:T(8,128)(2,1)} %bitcast.13), calls=%async_computation.3 | async-start | bytes 262144 | tf_op jit(solution)/shard_map/all_to_all | solution.py:72
  57.5 74.8 %all-to-all-start.1 = ((bf16[32,16,152]{2,1,0:T(8,128)(2,1)}), bf16[32,16,152]{2,1,0:T(8,128)(2,1)S(1)}, u32[]{:S(2)}, u32[]{:S(2)}) async-start(bf16[32,16,152]{2,1,0:T(8,128)(2,1)} %bitcast.3), calls=%async_computation.1 | async-start | bytes 524288 | tf_op jit(solution)/shard_map/all_to_all | solution.py:48
  112.3 15.4 %slice-start.4 = ((s8[5914624]{0:T(1024)(128)(4,1)}), s8[1720320]{0:T(1024)(128)(4,1)S(1)}, s32[]{:S(2)}) async-start(s8[5914624]{0:T(1024)(128)(4,1)} %bitcast.78), calls=%async_computation.8 | async-start | bytes 3440640
  117.6 5.2 %copy-start.2 = (bf16[32,79,152]{1,0,2:T(8,128)(2,1)S(1)}, bf16[32,79,152]{1,0,2:T(8,128)(2,1)}, u32[]{:S(2)}) copy-start(bf16[32,79,152]{1,0,2:T(8,128)(2,1)} %reshape.154) | copy-start | bytes 2305540
  117.6 10.0 %slice-start.5 = ((s8[5914624]{0:T(1024)(128)(4,1)}), s8[4194304]{0:T(1024)(128)(4,1)S(1)}, s32[]{:S(2)}) async-start(s8[5914624]{0:T(1024)(128)(4,1)} %bitcast.78), calls=%async_computation.9 | async-start | bytes 8388608
  117.6 10.0 %copy-start.3 = (bf16[32,79,152]{1,0,2:T(8,128)(2,1)S(1)}, bf16[32,79,152]{1,0,2:T(8,128)(2,1)}, u32[]{:S(2)}) copy-start(bf16[32,79,152]{1,0,2:T(8,128)(2,1)} %reshape.162) | copy-start | bytes 2305540
  117.6 12.0 %slice-start = ((s8[5914624]{0:T(1024)(128)(4,1)}), s8[4194304]{0:T(1024)(128)(4,1)S(1)}, s32[]{:S(2)}) async-start(s8[5914624]{0:T(1024)(128)(4,1)} %bitcast.74), calls=%async_computation.4 | async-start | bytes 8388608
  122.8 6.8 %slice-start.1 = ((s8[5914624]{0:T(1024)(128)(4,1)}), s8[1720320]{0:T(1024)(128)(4,1)S(1)}, s32[]{:S(2)}) async-start(s8[5914624]{0:T(1024)(128)(4,1)} %bitcast.74), calls=%async_computation.5 | async-start | bytes 3440640
  122.8 6.8 %copy-start.4 = (bf16[32,79,152]{1,0,2:T(8,128)(2,1)S(1)}, bf16[32,79,152]{1,0,2:T(8,128)(2,1)}, u32[]{:S(2)}) copy-start(bf16[32,79,152]{1,0,2:T(8,128)(2,1)} %reshape.170) | copy-start | bytes 2305540
  330.0 17.7 %slice-start.6 = ((s8[5914624]{0:T(1024)(128)(4,1)}), s8[1720320]{0:T(1024)(128)(4,1)S(1)}, s32[]{:S(2)}) async-start(s8[5914624]{0:T(1024)(128)(4,1)} %bitcast.80), calls=%async_computation.10 | async-start | bytes 3440640
  341.6 6.2 %slice-start.7 = ((s8[5914624]{0:T(1024)(128)(4,1)}), s8[4194304]{0:T(1024)(128)(4,1)S(1)}, s32[]{:S(2)}) async-start(s8[5914624]{0:T(1024)(128)(4,1)} %bitcast.80), calls=%async_computation.11 | async-start | bytes 8388608
  341.6 11.3 %slice-start.2 = ((s8[5914624]{0:T(1024)(128)(4,1)}), s8[4194304]{0:T(1024)(128)(4,1)S(1)}, s32[]{:S(2)}) async-start(s8[5914624]{0:T(1024)(128)(4,1)} %bitcast.76), calls=%async_computation.6 | async-start | bytes 8388608
  341.6 11.3 %slice-start.8 = ((s8[5603328]{0:T(1024)(128)(4,1)}), s8[4194304]{0:T(1024)(128)(4,1)S(1)}, s32[]{:S(2)}) async-start(s8[5603328]{0:T(1024)(128)(4,1)} %bitcast.82), calls=%async_computation.12 | async-start | bytes 8388608
  347.8 5.1 %slice-start.3 = ((s8[5914624]{0:T(1024)(128)(4,1)}), s8[1720320]{0:T(1024)(128)(4,1)S(1)}, s32[]{:S(2)}) async-start(s8[5914624]{0:T(1024)(128)(4,1)} %bitcast.76), calls=%async_computation.7 | async-start | bytes 3440640
  347.8 5.1 %slice-start.9 = ((s8[5603328]{0:T(1024)(128)(4,1)}), s8[1409024]{0:T(1024)(128)(4,1)S(1)}, s32[]{:S(2)}) async-start(s8[5603328]{0:T(1024)(128)(4,1)} %bitcast.82), calls=%async_computation.13 | async-start | bytes 2818048
  347.8 7.5 %copy-start.1 = (bf16[152,8,152]{2,1,0:T(8,128)(2,1)S(1)}, bf16[152,8,152]{2,1,0:T(8,128)(2,1)}, u32[]{:S(2)}) copy-start(bf16[152,8,152]{2,1,0:T(8,128)(2,1)} %param.12) | copy-start | bytes 1108996
where the time goes:
time: 363 us; the launch traced here: 356 us
  local copies, waits for them, and re-layouts  290 us (80%)
  matrix products  34.9 us (10%)
  starting transfers between devices  19.1 us (5%)
  waiting for transfers between devices  6.4 us (2%)
    gather x24, local copies, waits for them, and re-layouts, translate(): gathered = source_rows[entries[:, first_off:last_off]]  260 us
    dot_general x8, matrix products, translate(): jnp.einsum('tcb,abc->at', gathered, m2l_ops[:, :, first_off:last_off], pr...  34.2 us
    slice x1, local copies, waits for them, and re-layouts, translate(): m2l_ops[:, :, first_off:last_off]  22.2 us
  transfers between devices with their start and end apart: 4, of which 2 were waited for; matrix products, arithmetic and copies ran while one was open for 29% of the time, Pallas kernels for 0%

commit v1 on v0

v1 whole, which is shorter than its diff:
```python
import functools

import jax
import jax.numpy as jnp
from jax import lax
from jax.experimental import pallas as pl
from jax.experimental.pallas import tpu as pltpu
from jax.sharding import PartitionSpec as P

LANES = 128
BLANK = 1 << 20
AXES = ("leaf", "oct")


def ceil_to(n, m):
    return (n + m - 1) // m * m


def remap(entries, own, cap, shift_ref):
    slot = jnp.maximum(entries - own, 0)
    peer = slot // cap
    at = peer % LANES
    peers = shift_ref.shape[1]
    shift = jnp.zeros_like(entries)
    for k in range(peers // LANES):
        row = jnp.broadcast_to(shift_ref[:, k * LANES : (k + 1) * LANES], entries.shape)
        got = jnp.take_along_axis(row, at, axis=1, mode="promise_in_bounds")
        shift = jnp.where(peer // LANES == k, got, shift)
    column = jnp.where(entries < own, entries, entries - shift)
    return jnp.where(entries < 0, BLANK, column)


def prepare_kernel(
    fine_cap, coarse_cap, m_ref, lf_ref, lc_ref, sf_ref, sc_ref, mr_ref, idx_ref, scr
):
    surface, step_b, offsets = m_ref.shape
    fine_own, coarse_own = lf_ref.shape[0], lc_ref.shape[0]
    width = idx_ref.shape[1]

    @pl.when(pl.program_id(0) == 0)
    def _():
        scr[...] = jnp.zeros_like(scr)
        for first in range(0, offsets, LANES):
            size = min(LANES, offsets - first)
            for ref, own, cap, shift_ref, row in (
                (lf_ref, fine_own, fine_cap, sf_ref, 0),
                (lc_ref, coarse_own, coarse_cap, sc_ref, fine_own),
            ):
                entries = ref[:, first : first + size]
                if size < LANES:
                    blank = jnp.full((own, LANES - size), -1, jnp.int32)
                    entries = jnp.concatenate([entries, blank], axis=1)
                idx_ref[row : row + own, first : first + LANES] = remap(
                    entries, own, cap, shift_ref
                )

    for half in range(step_b // 8):
        for tile, first in enumerate(range(0, offsets, LANES)):
            size = min(LANES, offsets - first)
            block = m_ref[:, half * 8 : half * 8 + 8, first : first + size]
            scr[tile, :, 0:size] = block.astype(jnp.float32).reshape(surface * 8, size)
        for j in range(8):
            pair, side = half * 4 + j // 2, j % 2
            for tile in range(width // LANES):
                rows = scr[tile, pl.ds(j, surface, stride=8), :]
                at = side * width + tile * LANES
                mr_ref[pair, :, at : at + LANES] = rows.astype(jnp.bfloat16)


def prepare(m2l_ops, list_fine, list_coarse, shift_fine, shift_coarse, fine_cap, coarse_cap):
    surface, _, offsets = m2l_ops.shape
    width = ceil_to(offsets, LANES)
    targets = list_fine.shape[0] + list_coarse.shape[0]
    step_b = 16
    whole = lambda x: pl.BlockSpec(x.shape, lambda i: (0,) * x.ndim)
    return pl.pallas_call(
        functools.partial(prepare_kernel, fine_cap, coarse_cap),
        grid=(pl.cdiv(surface, step_b),),
        in_specs=[
            pl.BlockSpec((surface, step_b, offsets), lambda i: (0, i, 0)),
            whole(list_fine),
            whole(list_coarse),
            whole(shift_fine),
            whole(shift_coarse),
        ],
        out_specs=[
            pl.BlockSpec((step_b // 2, surface, 2 * width), lambda i: (i, 0, 0)),
            pl.BlockSpec((targets, width), lambda i: (0, 0)),
        ],
        out_shape=[
            jax.ShapeDtypeStruct((surface // 2, surface, 2 * width), jnp.bfloat16),
            jax.ShapeDtypeStruct((targets, width), jnp.int32),
        ],
        scratch_shapes=[pltpu.VMEM((width // LANES, surface * 8, LANES), jnp.float32)],
        compiler_params=pltpu.CompilerParams(vmem_limit_bytes=32 << 20),
        cost_estimate=pl.CostEstimate(
            flops=0, bytes_accessed=4 * surface * surface * width, transcendentals=0
        ),
        name="prepare",
    )(m2l_ops, list_fine, list_coarse, shift_fine, shift_coarse)


def gathered(idx, table_ref, pair, tiles):
    at = idx & (LANES - 1)
    value = None
    for k in range(tiles):
        row = table_ref[pair : pair + 1, k * LANES : (k + 1) * LANES]
        row = jnp.broadcast_to(row, idx.shape)
        got = jnp.take_along_axis(row, at, axis=1, mode="promise_in_bounds")
        value = got if k == 0 else jnp.where(idx >= k * LANES, got, value)
    return jnp.where(idx >= BLANK, 0, value)


def translate_kernel(fine_own, variants, pick_ref, idx_ref, tf_ref, tc_ref, m_ref, o_ref, g_ref):
    pairs, surface, width2 = m_ref.shape
    width = width2 // 2
    targets = idx_ref.shape[0]
    step = pl.program_id(0)

    @pl.when(step == 0)
    def _():
        o_ref[...] = jnp.zeros_like(o_ref)

    def work(fine_tiles, coarse_tiles):
        for q in range(pairs):
            for first in range(0, width, LANES):
                for low, high, table, tiles in (
                    (0, fine_own, tf_ref, fine_tiles),
                    (fine_own, targets, tc_ref, coarse_tiles),
                ):
                    idx = idx_ref[low:high, first : first + LANES]
                    both = gathered(idx, table, q, tiles)
                    g_ref[q, low:high, first : first + LANES] = (
                        (both << 16).astype(jnp.float32).astype(jnp.bfloat16)
                    )
                    g_ref[q, low:high, width + first : width + first + LANES] = both.astype(
                        jnp.float32
                    ).astype(jnp.bfloat16)
            o_ref[...] += lax.dot_general(
                m_ref[q],
                g_ref[q],
                (((1,), (1,)), ((), ())),
                preferred_element_type=jnp.float32,
            )

    for at, (fine_tiles, coarse_tiles) in enumerate(variants):
        pl.when(pick_ref[0] == at)(functools.partial(work, fine_tiles, coarse_tiles))


def translate(operators, idx, table_fine, table_coarse, pick, variants, fine_own):
    pairs_all, surface, width2 = operators.shape
    targets, width = idx.shape
    pairs = 4 if pairs_all % 4 == 0 else 1
    table_fine = table_fine.reshape(-1, pairs, table_fine.shape[1])
    table_coarse = table_coarse.reshape(-1, pairs, table_coarse.shape[1])
    whole = lambda x: pl.BlockSpec(x.shape, lambda i, s: (0,) * x.ndim)
    rows = lambda x: pl.BlockSpec((None,) + x.shape[1:], lambda i, s: (i, 0, 0))
    return pl.pallas_call(
        functools.partial(translate_kernel, fine_own, variants),
        grid_spec=pltpu.PrefetchScalarGridSpec(
            num_scalar_prefetch=1,
            grid=(pairs_all // pairs,),
            in_specs=[
                whole(idx),
                rows(table_fine),
                rows(table_coarse),
                pl.BlockSpec((pairs, surface, width2), lambda i, s: (i, 0, 0)),
            ],
            out_specs=pl.BlockSpec((surface, targets), lambda i, s: (0, 0)),
            scratch_shapes=[pltpu.VMEM((pairs, targets, width2), jnp.bfloat16)],
        ),
        out_shape=jax.ShapeDtypeStruct((surface, targets), jnp.float32),
        compiler_params=pltpu.CompilerParams(vmem_limit_bytes=32 << 20),
        cost_estimate=pl.CostEstimate(
            flops=2 * pairs_all * surface * targets * width2,
            bytes_accessed=2 * pairs_all * surface * width2,
            transcendentals=0,
        ),
        name="translate",
    )(pick, idx, table_fine, table_coarse, operators)


def offsets_of(asks):
    peers, cap = asks.shape
    counts = jnp.sum((asks >= 0).astype(jnp.int32), axis=1)
    order = jnp.arange(peers, dtype=jnp.int32)
    before = jnp.sum(jnp.where(order[None, :] < order[:, None], counts[None, :], 0), axis=1)
    shift = order * cap - before
    place = before[:, None] + jnp.arange(cap, dtype=jnp.int32)[None, :]
    place = jnp.where(asks >= 0, place, -1).reshape(-1)
    padded = jnp.pad(shift, (0, ceil_to(peers, LANES) - peers))[None, :]
    return padded, place, jnp.sum(counts)


def select_columns(arrived, place, count):
    hot = (place[:, None] == jnp.arange(count, dtype=jnp.int32)[None, :]).astype(jnp.bfloat16)
    return lax.dot_general(
        arrived, hot, (((0,), (0,)), ((), ())), preferred_element_type=jnp.float32
    )


def pack(table):
    surface, count = table.shape
    table = jnp.pad(table, ((0, 0), (0, ceil_to(count, LANES) - count)))
    peak = jnp.maximum(jnp.max(jnp.abs(table)), 1e-30)
    level = jnp.floor(jnp.log2(peak))
    fixed = jnp.round(table * jnp.exp2(13.0 - level)).astype(jnp.int32)
    fixed = fixed.reshape(surface // 2, 2, -1)
    return fixed[:, 1] * 65536 + fixed[:, 0], jnp.exp2(level - 29.0)


def exchange(x):
    return lax.all_to_all(x, AXES, split_axis=0, concat_axis=0, tiled=True)


def body(
    dens_fine, parent, child_code, m2m_ops, m2l_ops, ask_fine, list_fine, ask_coarse, list_coarse
):
    surface, fine_own = dens_fine.shape
    coarse_own = list_coarse.shape[0]
    asks_fine, asks_coarse = ask_fine[0], ask_coarse[0]
    peers, fine_cap = asks_fine.shape
    coarse_cap = asks_coarse.shape[1]
    wanted = exchange(
        jnp.concatenate(
            [asks_fine, jnp.where(asks_coarse < 0, -1, asks_coarse + fine_own)], axis=1
        )
    )

    shift_fine, place_fine, used_fine = offsets_of(asks_fine)
    shift_coarse, place_coarse, used_coarse = offsets_of(asks_coarse)
    operators, idx = prepare(
        m2l_ops, list_fine, list_coarse, shift_fine, shift_coarse, fine_cap, coarse_cap
    )

    positions = jnp.arange(8, dtype=jnp.int32)
    spread = jnp.where(
        (child_code[None, :] == positions[:, None])[:, None, :],
        dens_fine[None],
        jnp.zeros((), jnp.bfloat16),
    )
    child_terms = jnp.dot(
        m2m_ops.reshape(surface, 8 * surface),
        spread.reshape(8 * surface, fine_own),
        preferred_element_type=jnp.float32,
    )
    local_parent = parent - lax.axis_index(AXES) * coarse_own
    members = (local_parent[:, None] == jnp.arange(coarse_own, dtype=jnp.int32)[None, :]).astype(
        jnp.float32
    )
    dens_coarse = jnp.dot(child_terms, members, precision=lax.Precision.HIGHEST).astype(
        jnp.bfloat16
    )

    own = jnp.concatenate([dens_fine, dens_coarse], axis=1)
    picked = (
        wanted.reshape(-1)[:, None] == jnp.arange(fine_own + coarse_own, dtype=jnp.int32)[None, :]
    ).astype(jnp.bfloat16)
    outgoing = lax.dot_general(
        picked, own, (((1,), (1,)), ((), ())), preferred_element_type=jnp.float32
    ).astype(jnp.bfloat16)
    arrived = exchange(outgoing.reshape(peers, fine_cap + coarse_cap, surface))

    remote_fine = (peers - 1) * fine_cap
    remote_coarse = (peers - 1) * coarse_cap
    came_fine = select_columns(
        arrived[:, :fine_cap].reshape(-1, surface), place_fine, remote_fine
    )
    came_coarse = select_columns(
        arrived[:, fine_cap:].reshape(-1, surface), place_coarse, remote_coarse
    )
    table_fine, unit_fine = pack(
        jnp.concatenate([dens_fine.astype(jnp.float32), came_fine], axis=1)
    )
    table_coarse, unit_coarse = pack(
        jnp.concatenate([dens_coarse.astype(jnp.float32), came_coarse], axis=1)
    )
    all_fine = table_fine.shape[1] // LANES
    all_coarse = table_coarse.shape[1] // LANES
    need_fine = (fine_own + used_fine + LANES - 1) // LANES
    need_coarse = (coarse_own + used_coarse + LANES - 1) // LANES
    variants = [(min(3, all_fine), min(2, all_coarse)), (min(4, all_fine), min(2, all_coarse))]
    variants = variants + [(all_fine, all_coarse)]
    pick = jnp.int32(len(variants) - 1)
    for at in reversed(range(len(variants) - 1)):
        fits = (need_fine <= variants[at][0]) & (need_coarse <= variants[at][1])
        pick = jnp.where(fits, at, pick)
    both = translate(
        operators, idx, table_fine, table_coarse, pick.reshape(1), variants, fine_own
    )
    return both[:, :fine_own] * unit_fine, both[:, fine_own:] * (0.5 * unit_coarse)


def solution(mesh):
    return jax.shard_map(
        body,
        mesh=mesh,
        in_specs=(
            P(None, AXES),
            P(AXES),
            P(AXES),
            P(),
            P(),
            P(AXES, None, None),
            P(AXES, None),
            P(AXES, None, None),
            P(AXES, None),
        ),
        out_specs=(P(None, AXES), P(None, AXES)),
        check_vma=False,
    )
```

time: 363 us -> 123 us (0.34)
  the two profiles are of different devices: /device:TPU:8 before, /device:TPU:25 now
where the time goes in v1:
time: 123 us; the launch traced here: 122 us
  Pallas kernels  74.8 us (61%)
  local copies, waits for them, and re-layouts  20.7 us (17%)
  starting transfers between devices  12 us (10%)
  other arithmetic  7.13 us (6%)
  between operations  3.83 us (3%)
  matrix products  3.56 us (3%)
    pallas_call x1, Pallas kernels, translate(): pl.pallas_call(functools.partial(translate_kernel, fine_own, variants), g...  58.8 us
    unnamed x15, local copies, waits for them, and re-layouts  17.9 us
    pallas_call x1, Pallas kernels, prepare(): pl.pallas_call(functools.partial(prepare_kernel, fine_cap, coarse_cap), g...  16.1 us
    all_to_all x2, starting transfers between devices, exchange(): return lax.all_to_all(x, AXES, split_axis=0, concat_axis=0, tiled=True)  12 us
  transfers between devices with their start and end apart: 2, of which 0 were waited for; matrix products, arithmetic and copies ran while one was open for 5% of the time, Pallas kernels for 13%

profile of v1, /device:TPU:25, one launch (start us, length us, event | category | flops | bytes accessed | tf_op | source)
XLA Modules:
  0.0 122.1 jit_solution(13451052006997431494)
XLA Ops:
  0.6 0.8 copy.48
  1.5 0.8 copy.49
  2.2 0.7 convert_reduce_fusion
  3.0 0.7 pad_add_fusion
  3.6 6.2 %all-to-all-start = ((s32[32,1,24]{2,1,0:T(1,128)}), s32[32,1,24]{2,1,0:T(1,128)S(1)}, u32[]{:S(2)}, u32[]{:S(2)}) async-start(s32[32,1,24]{2,1,0:T(1,128)} %bitcast.5), calls=%async_computation | async-start | bytes 32768 | tf_op jit(solution)/shard_map/all_to_all | solution.py:213
  9.8 0.7 broadcast_compare_fusion.2
  10.5 0.6 convert_reduce_fusion.2
  11.4 0.7 iota_compare_fusion.10
  12.2 0.7 broadcast_subtract_fusion
  12.9 1.3 %convolution_bitcast_fusion = f32[144,152]{1,0:T(8,128)S(1)} fusion(bf16[152,8,152]{2,1,0:T(8,128)(2,1)S(1)} %copy-done, pred[8,144]{1,0:T(8,128)(4,1)S(1)} %iota_compare_fusion.10, bf16[152,144]{0,1:T(8,128)(2,1)} %param.9), kind=kOutput, calls=%fused_computation.1 | convolution fusion | flops 53406720 | bytes 502144 | tf_op jit(solution)/shard_map/dot_general | solution.py:242
  14.2 0.3 convolution_convert_fusion.1
  14.6 0.5 broadcast.91
  15.1 0.7 reduce.7
  15.8 1.3 %convolution_convert_fusion = bf16[768,152]{0,1:T(8,128)(2,1)S(1)} fusion(s32[768]{0:T(1024)S(1)} %eq.71, bf16[152,32]{0,1:T(8,128)(2,1)S(1)} %convolution_convert_fusion.1, bf16[152,144]{0,1:T(8,128)(2,1)} %param.9), kind=kOutput, calls=%fused_computation | convolution fusion | flops 41449984 | bytes 290048 | tf_op jit(solution)/shard_map/dot_general | solution.py:259
  17.2 0.9 copy.54
  18.1 5.8 %all-to-all-start.1 = ((bf16[32,24,152]{2,1,0:T(8,128)(2,1)}), bf16[32,24,152]{2,1,0:T(8,128)(2,1)S(1)}, u32[]{:S(2)}, u32[]{:S(2)}) async-start(bf16[32,24,152]{2,1,0:T(8,128)(2,1)} %bitcast.7), calls=%async_computation.1 | async-start | bytes 786432 | tf_op jit(solution)/shard_map/all_to_all | solution.py:213
  25.3 1.0 copy.50
  27.0 0.9 copy-done.3
  27.9 0.8 copy-done.4
  28.7 16.1 %prepare.1 = (bf16[76,152,768]{2,1,0:T(8,128)(2,1)S(1)}, s32[176,384]{1,0:T(8,128)S(1)}) custom-call(bf16[152,152,316]{2,1,0:T(8,128)(2,1)} %m_ref.1, s32[144,316]{1,0:T(8,128)S(1)} %copy-done.3, s32[32,316]{1,0:T(8,128)S(1)} %copy-done.4, s32[1,128]{1,0:T(1,128)S(1)} %get-tuple-element.23.sf_ref, s32[1,128]{1,0:T(1,128)S(1)} %get-tuple-element.22.sc_ref), custom_call_target="tpu_custom_call" | custom-call | bytes 35487744 | tf_op jit(solution)/shard_map/prepare/pallas_call | solution.py:76
  44.8 6.1 %copy-done.1 = bf16[76,152,768]{2,1,0:T(8,128)(2,1)} copy-done((bf16[76,152,768]{2,1,0:T(8,128)(2,1)}, bf16[76,152,768]{2,1,0:T(8,128)(2,1)S(1)}, u32[]{:S(2)}) %copy-start.1) | copy-done | bytes 17743896
  50.9 0.3 fusion.11
  51.2 0.7 abs_reduce_fusion
  52.6 0.4 fusion
  53.0 0.8 fusion.8
  54.5 0.2 concatenate.22
  55.1 0.2 fusion.19
  55.5 0.2 fusion.6
  55.8 6.0 %copy-done.2 = bf16[76,152,768]{2,1,0:T(8,128)(2,1)S(1)} copy-done((bf16[76,152,768]{2,1,0:T(8,128)(2,1)S(1)}, bf16[76,152,768]{2,1,0:T(8,128)(2,1)}, u32[]{:S(2)}) %copy-start.2) | copy-done | bytes 17743896
  61.8 58.8 %translate.1 = f32[152,176]{1,0:T(8,128)S(1)} custom-call(s32[1]{0:T(128)} %bitcast.1.pick_ref, s32[176,384]{1,0:T(8,128)S(1)} %get-tuple-element.4.idx_ref, s32[19,4,640]{2,1,0:T(4,128)S(1)} %add.96.tf_ref, s32[19,4,384]{2,1,0:T(4,128)S(1)} %add.102.tc_ref, bf16[76,152,768]{2,1,0:T(8,128)(2,1)S(1)} %copy-done.2), custom_call_target="tpu_custom_call" | custom-call | flops 3122921472 | bytes 17743872 | tf_op jit(solution)/shard_map/translate/pallas_call | solution.py:158
  120.6 0.7 copy.62
  121.4 0.8 copy.61
  (37 shorter events, 1.7 us)
Async XLA Ops:
  0.6 12.3 %copy-start = (bf16[152,8,152]{2,1,0:T(8,128)(2,1)S(1)}, bf16[152,8,152]{2,1,0:T(8,128)(2,1)}, u32[]{:S(2)}) copy-start(bf16[152,8,152]{2,1,0:T(8,128)(2,1)} %param.12) | copy-start | bytes 1108996
  3.6 10.9 %all-to-all-start = ((s32[32,1,24]{2,1,0:T(1,128)}), s32[32,1,24]{2,1,0:T(1,128)S(1)}, u32[]{:S(2)}, u32[]{:S(2)}) async-start(s32[32,1,24]{2,1,0:T(1,128)} %bitcast.5), calls=%async_computation | async-start | bytes 32768 | tf_op jit(solution)/shard_map/all_to_all | solution.py:213
  18.1 32.8 %all-to-all-start.1 = ((bf16[32,24,152]{2,1,0:T(8,128)(2,1)}), bf16[32,24,152]{2,1,0:T(8,128)(2,1)S(1)}, u32[]{:S(2)}, u32[]{:S(2)}) async-start(bf16[32,24,152]{2,1,0:T(8,128)(2,1)} %bitcast.7), calls=%async_computation.1 | async-start | bytes 786432 | tf_op jit(solution)/shard_map/all_to_all | solution.py:213
  27.0 0.9 copy-start.3
  27.9 0.8 copy-start.4
  44.8 6.1 %copy-start.1 = (bf16[76,152,768]{2,1,0:T(8,128)(2,1)}, bf16[76,152,768]{2,1,0:T(8,128)(2,1)S(1)}, u32[]{:S(2)}) copy-start(bf16[76,152,768]{2,1,0:T(8,128)(2,1)S(1)} %get-tuple-element.5.m_ref) | copy-start | bytes 53231620
  55.7 6.0 %copy-start.2 = (bf16[76,152,768]{2,1,0:T(8,128)(2,1)S(1)}, bf16[76,152,768]{2,1,0:T(8,128)(2,1)}, u32[]{:S(2)}) copy-start(bf16[76,152,768]{2,1,0:T(8,128)(2,1)} %copy-done.1) | copy-start | bytes 53231620

commit v2 on v1

--- a/solution.py
+++ b/solution.py
@@ -8,6 +8,7 @@
 from jax.sharding import PartitionSpec as P
 
 LANES = 128
+CHUNK = 16
 BLANK = 1 << 20
 AXES = ("leaf", "oct")
 
@@ -60,11 +61,10 @@
             block = m_ref[:, half * 8 : half * 8 + 8, first : first + size]
             scr[tile, :, 0:size] = block.astype(jnp.float32).reshape(surface * 8, size)
         for j in range(8):
-            pair, side = half * 4 + j // 2, j % 2
             for tile in range(width // LANES):
                 rows = scr[tile, pl.ds(j, surface, stride=8), :]
-                at = side * width + tile * LANES
-                mr_ref[pair, :, at : at + LANES] = rows.astype(jnp.bfloat16)
+                at = j * width + tile * LANES
+                mr_ref[half, :, at : at + LANES] = rows.astype(jnp.bfloat16)
 
 
 def prepare(m2l_ops, list_fine, list_coarse, shift_fine, shift_coarse, fine_cap, coarse_cap):
@@ -84,15 +84,15 @@
             whole(shift_coarse),
         ],
         out_specs=[
-            pl.BlockSpec((step_b // 2, surface, 2 * width), lambda i: (i, 0, 0)),
+            pl.BlockSpec((step_b // 8, surface, 8 * width), lambda i: (i, 0, 0)),
             pl.BlockSpec((targets, width), lambda i: (0, 0)),
         ],
         out_shape=[
-            jax.ShapeDtypeStruct((surface // 2, surface, 2 * width), jnp.bfloat16),
+            jax.ShapeDtypeStruct((surface // 8, surface, 8 * width), jnp.bfloat16),
             jax.ShapeDtypeStruct((targets, width), jnp.int32),
         ],
         scratch_shapes=[pltpu.VMEM((width // LANES, surface * 8, LANES), jnp.float32)],
-        compiler_params=pltpu.CompilerParams(vmem_limit_bytes=32 << 20),
+        compiler_params=pltpu.CompilerParams(vmem_limit_bytes=56 << 20),
         cost_estimate=pl.CostEstimate(
             flops=0, bytes_accessed=4 * surface * surface * width, transcendentals=0
         ),
@@ -100,21 +100,9 @@
     )(m2l_ops, list_fine, list_coarse, shift_fine, shift_coarse)
 
 
-def gathered(idx, table_ref, pair, tiles):
-    at = idx & (LANES - 1)
-    value = None
-    for k in range(tiles):
-        row = table_ref[pair : pair + 1, k * LANES : (k + 1) * LANES]
-        row = jnp.broadcast_to(row, idx.shape)
-        got = jnp.take_along_axis(row, at, axis=1, mode="promise_in_bounds")
-        value = got if k == 0 else jnp.where(idx >= k * LANES, got, value)
-    return jnp.where(idx >= BLANK, 0, value)
-
-
 def translate_kernel(fine_own, variants, pick_ref, idx_ref, tf_ref, tc_ref, m_ref, o_ref, g_ref):
-    pairs, surface, width2 = m_ref.shape
-    width = width2 // 2
-    targets = idx_ref.shape[0]
+    targets, width = idx_ref.shape
+    pairs = m_ref.shape[1] // (2 * width)
     step = pl.program_id(0)
 
     @pl.when(step == 0)
@@ -122,58 +110,62 @@
         o_ref[...] = jnp.zeros_like(o_ref)
 
     def work(fine_tiles, coarse_tiles):
-        for q in range(pairs):
-            for first in range(0, width, LANES):
-                for low, high, table, tiles in (
-                    (0, fine_own, tf_ref, fine_tiles),
-                    (fine_own, targets, tc_ref, coarse_tiles),
-                ):
-                    idx = idx_ref[low:high, first : first + LANES]
-                    both = gathered(idx, table, q, tiles)
-                    g_ref[q, low:high, first : first + LANES] = (
-                        (both << 16).astype(jnp.float32).astype(jnp.bfloat16)
+        for first in range(0, width, LANES):
+            for low in range(0, targets, CHUNK):
+                table, tiles = (tf_ref, fine_tiles) if low < fine_own else (tc_ref, coarse_tiles)
+                idx = idx_ref[low : low + CHUNK, first : first + LANES]
+                at = idx & (LANES - 1)
+                later = [idx >= k * LANES for k in range(1, tiles)]
+                blank = idx >= BLANK
+                for q in range(pairs):
+                    value = None
+                    for k in range(tiles):
+                        row = table[q : q + 1, k * LANES : (k + 1) * LANES]
+                        row = jnp.broadcast_to(row, idx.shape)
+                        got = jnp.take_along_axis(row, at, axis=1, mode="promise_in_bounds")
+                        value = got if k == 0 else jnp.where(later[k - 1], got, value)
+                    value = jnp.where(blank, 0, value)
+                    to = 2 * q * width + first
+                    g_ref[low : low + CHUNK, to : to + LANES] = (
+                        (value << 16).astype(jnp.float32).astype(jnp.bfloat16)
                     )
-                    g_ref[q, low:high, width + first : width + first + LANES] = both.astype(
-                        jnp.float32
-                    ).astype(jnp.bfloat16)
-            o_ref[...] += lax.dot_general(
-                m_ref[q],
-                g_ref[q],
-                (((1,), (1,)), ((), ())),
-                preferred_element_type=jnp.float32,
-            )
+                    to = to + width
+                    g_ref[low : low + CHUNK, to : to + LANES] = value.astype(jnp.float32).astype(
+                        jnp.bfloat16
+                    )
+        o_ref[...] += lax.dot_general(
+            m_ref[...],
+            g_ref[...],
+            (((1,), (1,)), ((), ())),
+            preferred_element_type=jnp.float32,
+        )
 
     for at, (fine_tiles, coarse_tiles) in enumerate(variants):
         pl.when(pick_ref[0] == at)(functools.partial(work, fine_tiles, coarse_tiles))
 
 
 def translate(operators, idx, table_fine, table_coarse, pick, variants, fine_own):
-    pairs_all, surface, width2 = operators.shape
+    blocks, surface, depth = operators.shape
     targets, width = idx.shape
-    pairs = 4 if pairs_all % 4 == 0 else 1
-    table_fine = table_fine.reshape(-1, pairs, table_fine.shape[1])
-    table_coarse = table_coarse.reshape(-1, pairs, table_coarse.shape[1])
+    pairs = depth // (2 * width)
+    table_fine = table_fine.reshape(blocks, pairs, table_fine.shape[1])
+    table_coarse = table_coarse.reshape(blocks, pairs, table_coarse.shape[1])
     whole = lambda x: pl.BlockSpec(x.shape, lambda i, s: (0,) * x.ndim)
     rows = lambda x: pl.BlockSpec((None,) + x.shape[1:], lambda i, s: (i, 0, 0))
     return pl.pallas_call(
         functools.partial(translate_kernel, fine_own, variants),
         grid_spec=pltpu.PrefetchScalarGridSpec(
             num_scalar_prefetch=1,
-            grid=(pairs_all // pairs,),
-            in_specs=[
-                whole(idx),
-                rows(table_fine),
-                rows(table_coarse),
-                pl.BlockSpec((pairs, surface, width2), lambda i, s: (i, 0, 0)),
-            ],
+            grid=(blocks,),
+            in_specs=[whole(idx), rows(table_fine), rows(table_coarse), rows(operators)],
             out_specs=pl.BlockSpec((surface, targets), lambda i, s: (0, 0)),
-            scratch_shapes=[pltpu.VMEM((pairs, targets, width2), jnp.bfloat16)],
+            scratch_shapes=[pltpu.VMEM((targets, depth), jnp.bfloat16)],
         ),
         out_shape=jax.ShapeDtypeStruct((surface, targets), jnp.float32),
-        compiler_params=pltpu.CompilerParams(vmem_limit_bytes=32 << 20),
+        compiler_params=pltpu.CompilerParams(vmem_limit_bytes=56 << 20),
         cost_estimate=pl.CostEstimate(
-            flops=2 * pairs_all * surface * targets * width2,
-            bytes_accessed=2 * pairs_all * surface * width2,
+            flops=2 * blocks * surface * targets * depth,
+            bytes_accessed=2 * blocks * surface * depth,
             transcendentals=0,
         ),
         name="translate",

time: 123 us -> 109 us (0.89)
  the two profiles are of different devices: /device:TPU:25 before, /device:TPU:3 now
where the time goes in v2:
time: 109 us; the launch traced here: 108 us
  Pallas kernels  71 us (65%)
  starting transfers between devices  11.5 us (11%)
  other arithmetic  8.91 us (8%)
  local copies, waits for them, and re-layouts  8.83 us (8%)
  between operations  3.76 us (3%)
  matrix products  3.56 us (3%)
    pallas_call x1, Pallas kernels, translate(): pl.pallas_call(functools.partial(translate_kernel, fine_own, variants), g...  51.2 us
    pallas_call x1, Pallas kernels, prepare(): pl.pallas_call(functools.partial(prepare_kernel, fine_cap, coarse_cap), g...  19.8 us
    all_to_all x2, starting transfers between devices, exchange(): return lax.all_to_all(x, AXES, split_axis=0, concat_axis=0, tiled=True)  11.5 us
    unnamed x7, local copies, waits for them, and re-layouts  4.05 us
  transfers between devices with their start and end apart: 2, of which 1 were waited for; matrix products, arithmetic and copies ran while one was open for 6% of the time, Pallas kernels for 18%

profile of v2, /device:TPU:3, one launch (start us, length us, event | category | flops | bytes accessed | tf_op | source)
XLA Modules:
  0.0 108.3 jit_solution(124877738151647246)
XLA Ops:
  0.6 0.8 copy.48
  1.5 0.8 copy.49
  2.2 0.7 convert_reduce_fusion
  2.9 0.7 pad_add_fusion
  3.6 6.4 %all-to-all-start = ((s32[32,1,24]{2,1,0:T(1,128)}), s32[32,1,24]{2,1,0:T(1,128)S(1)}, u32[]{:S(2)}, u32[]{:S(2)}) async-start(s32[32,1,24]{2,1,0:T(1,128)} %bitcast.5), calls=%async_computation | async-start | bytes 32768 | tf_op jit(solution)/shard_map/all_to_all | solution.py:205
  10.1 0.7 broadcast_compare_fusion.2
  10.8 0.6 convert_reduce_fusion.2
  11.6 0.7 iota_compare_fusion.10
  12.5 0.7 broadcast_subtract_fusion
  13.2 1.3 %convolution_bitcast_fusion = f32[144,152]{1,0:T(8,128)S(1)} fusion(bf16[152,8,152]{2,1,0:T(8,128)(2,1)S(1)} %copy-done, pred[8,144]{1,0:T(8,128)(4,1)S(1)} %iota_compare_fusion.10, bf16[152,144]{0,1:T(8,128)(2,1)} %param.9), kind=kOutput, calls=%fused_computation.1 | convolution fusion | flops 53406720 | bytes 502144 | tf_op jit(solution)/shard_map/dot_general | solution.py:234
  14.5 0.3 convolution_convert_fusion.1
  14.8 0.8 all-to-all-done
  15.6 0.5 broadcast.91
  16.1 0.7 reduce.7
  16.9 1.3 %convolution_convert_fusion = bf16[768,152]{0,1:T(8,128)(2,1)S(1)} fusion(s32[768]{0:T(1024)S(1)} %eq.71, bf16[152,32]{0,1:T(8,128)(2,1)S(1)} %convolution_convert_fusion.1, bf16[152,144]{0,1:T(8,128)(2,1)} %param.9), kind=kOutput, calls=%fused_computation | convolution fusion | flops 41449984 | bytes 290048 | tf_op jit(solution)/shard_map/dot_general | solution.py:251
  18.2 0.9 copy.54
  19.1 5.0 %all-to-all-start.1 = ((bf16[32,24,152]{2,1,0:T(8,128)(2,1)}), bf16[32,24,152]{2,1,0:T(8,128)(2,1)S(1)}, u32[]{:S(2)}, u32[]{:S(2)}) async-start(bf16[32,24,152]{2,1,0:T(8,128)(2,1)} %bitcast.7), calls=%async_computation.1 | async-start | bytes 786432 | tf_op jit(solution)/shard_map/all_to_all | solution.py:205
  24.2 0.6 pad_bitcast_fusion
  26.1 1.0 copy.50
  27.8 19.8 %prepare.1 = (bf16[19,152,3072]{2,1,0:T(8,128)(2,1)}, s32[176,384]{1,0:T(8,128)}) custom-call(bf16[152,152,316]{2,1,0:T(8,128)(2,1)} %m_ref.1, s32[144,316]{1,0:T(8,128)} %lf_ref.1, s32[32,316]{1,0:T(8,128)} %lc_ref.1, s32[1,128]{1,0:T(1,128)} %get-tuple-element.23.sf_ref, s32[1,128]{1,0:T(1,128)} %get-tuple-element.22.sc_ref), custom_call_target="tpu_custom_call" | custom-call | bytes 35487744 | tf_op jit(solution)/shard_map/prepare/pallas_call | solution.py:76
  47.6 0.3 fusion.11
  47.8 0.7 abs_reduce_fusion
  49.3 0.4 fusion
  49.7 0.8 fusion.8
  51.2 0.2 concatenate.22
  52.0 0.7 add.102.tc_ref
  53.0 0.7 add.96.tf_ref
  53.7 51.2 %translate.1 = f32[152,176]{1,0:T(8,128)} custom-call(s32[1]{0:T(128)} %bitcast.1.pick_ref, s32[176,384]{1,0:T(8,128)} %get-tuple-element.4.idx_ref, s32[19,4,640]{2,1,0:T(4,128)} %add.96.tf_ref, s32[19,4,384]{2,1,0:T(4,128)} %add.102.tc_ref, bf16[19,152,3072]{2,1,0:T(8,128)(2,1)} %get-tuple-element.5.m_ref), custom_call_target="tpu_custom_call" | custom-call | flops 3122921472 | bytes 17743872 | tf_op jit(solution)/shard_map/translate/pallas_call | solution.py:155
  104.9 1.0 slice_multiply_fusion.2
  105.9 0.7 copy.62
  106.6 0.9 slice_multiply_fusion.1
  107.5 0.8 copy.61
  (29 shorter events, 1.9 us)
Async XLA Ops:
  0.6 12.5 %copy-start = (bf16[152,8,152]{2,1,0:T(8,128)(2,1)S(1)}, bf16[152,8,152]{2,1,0:T(8,128)(2,1)}, u32[]{:S(2)}) copy-start(bf16[152,8,152]{2,1,0:T(8,128)(2,1)} %param.12) | copy-start | bytes 1108996
  3.6 12.0 %all-to-all-start = ((s32[32,1,24]{2,1,0:T(1,128)}), s32[32,1,24]{2,1,0:T(1,128)S(1)}, u32[]{:S(2)}, u32[]{:S(2)}) async-start(s32[32,1,24]{2,1,0:T(1,128)} %bitcast.5), calls=%async_computation | async-start | bytes 32768 | tf_op jit(solution)/shard_map/all_to_all | solution.py:205
  19.1 28.5 %all-to-all-start.1 = ((bf16[32,24,152]{2,1,0:T(8,128)(2,1)}), bf16[32,24,152]{2,1,0:T(8,128)(2,1)S(1)}, u32[]{:S(2)}, u32[]{:S(2)}) async-start(bf16[32,24,152]{2,1,0:T(8,128)(2,1)} %bitcast.7), calls=%async_computation.1 | async-start | bytes 786432 | tf_op jit(solution)/shard_map/all_to_all | solution.py:205

commit v3 on v2

--- a/solution.py
+++ b/solution.py
@@ -184,11 +184,18 @@
     return padded, place, jnp.sum(counts)
 
 
-def select_columns(arrived, place, count):
-    hot = (place[:, None] == jnp.arange(count, dtype=jnp.int32)[None, :]).astype(jnp.bfloat16)
-    return lax.dot_general(
-        arrived, hot, (((0,), (0,)), ((), ())), preferred_element_type=jnp.float32
-    )
+def sources_of(asks, place, own, count):
+    peers = asks.shape[0]
+    octant = (asks + own * jnp.arange(peers, dtype=jnp.int32)[:, None]).reshape(-1)
+    columns = jnp.arange(count, dtype=jnp.int32)
+    hit = place[None, :] == columns[:, None]
+    return jnp.sum(jnp.where(hit, octant[None, :] + 1, 0), axis=1) - 1
+
+
+def select_columns(rows, sources):
+    octants = jnp.arange(rows.shape[0], dtype=jnp.int32)
+    hot = (octants[:, None] == sources[None, :]).astype(jnp.bfloat16)
+    return lax.dot_general(rows, hot, (((0,), (0,)), ((), ())), preferred_element_type=jnp.float32)
 
 
 def pack(table):
@@ -201,10 +208,6 @@
     return fixed[:, 1] * 65536 + fixed[:, 0], jnp.exp2(level - 29.0)
 
 
-def exchange(x):
-    return lax.all_to_all(x, AXES, split_axis=0, concat_axis=0, tiled=True)
-
-
 def body(
     dens_fine, parent, child_code, m2m_ops, m2l_ops, ask_fine, list_fine, ask_coarse, list_coarse
 ):
@@ -213,11 +216,7 @@
     asks_fine, asks_coarse = ask_fine[0], ask_coarse[0]
     peers, fine_cap = asks_fine.shape
     coarse_cap = asks_coarse.shape[1]
-    wanted = exchange(
-        jnp.concatenate(
-            [asks_fine, jnp.where(asks_coarse < 0, -1, asks_coarse + fine_own)], axis=1
-        )
-    )
+    all_fine_rows = lax.all_gather(dens_fine.T, AXES, axis=0, tiled=True)
 
     shift_fine, place_fine, used_fine = offsets_of(asks_fine)
     shift_coarse, place_coarse, used_coarse = offsets_of(asks_coarse)
@@ -244,23 +243,14 @@
         jnp.bfloat16
     )
 
-    own = jnp.concatenate([dens_fine, dens_coarse], axis=1)
-    picked = (
-        wanted.reshape(-1)[:, None] == jnp.arange(fine_own + coarse_own, dtype=jnp.int32)[None, :]
-    ).astype(jnp.bfloat16)
-    outgoing = lax.dot_general(
-        picked, own, (((1,), (1,)), ((), ())), preferred_element_type=jnp.float32
-    ).astype(jnp.bfloat16)
-    arrived = exchange(outgoing.reshape(peers, fine_cap + coarse_cap, surface))
+    all_coarse_rows = lax.all_gather(dens_coarse.T, AXES, axis=0, tiled=True)
 
     remote_fine = (peers - 1) * fine_cap
     remote_coarse = (peers - 1) * coarse_cap
-    came_fine = select_columns(
-        arrived[:, :fine_cap].reshape(-1, surface), place_fine, remote_fine
-    )
-    came_coarse = select_columns(
-        arrived[:, fine_cap:].reshape(-1, surface), place_coarse, remote_coarse
-    )
+    from_fine = sources_of(asks_fine, place_fine, fine_own, remote_fine)
+    from_coarse = sources_of(asks_coarse, place_coarse, coarse_own, remote_coarse)
+    came_fine = select_columns(all_fine_rows, from_fine)
+    came_coarse = select_columns(all_coarse_rows, from_coarse)
     table_fine, unit_fine = pack(
         jnp.concatenate([dens_fine.astype(jnp.float32), came_fine], axis=1)
     )

time: 109 us -> 181 us (1.66)
  the two profiles are of different devices: /device:TPU:3 before, /device:TPU:10 now
where the time goes in v3:
time: 181 us; the launch traced here: 179 us
  Pallas kernels  70.9 us (39%)
  blocking collectives  68.6 us (38%)
  between operations  17.1 us (9%)
  other arithmetic  8.54 us (5%)
  local copies, waits for them, and re-layouts  7.4 us (4%)
  matrix products  5.5 us (3%)
    all_gather x1, blocking collectives, body(): all_coarse_rows = lax.all_gather(dens_coarse.T, AXES, axis=0, tiled=True)  68.6 us
    pallas_call x1, Pallas kernels, translate(): pl.pallas_call(functools.partial(translate_kernel, fine_own, variants), g...  51.2 us
    pallas_call x1, Pallas kernels, prepare(): pl.pallas_call(functools.partial(prepare_kernel, fine_cap, coarse_cap), g...  19.7 us
    unnamed x7, local copies, waits for them, and re-layouts  3.98 us
    dot_general x2, matrix products, select_columns(): lax.dot_general(rows, hot, (((0,), (0,)), ((), ())), preferred_element_ty...  3.92 us
  transfers between devices with their start and end apart: 1, of which 0 were waited for; matrix products, arithmetic and copies ran while one was open for 7% of the time, Pallas kernels for 11%

profile of v3, /device:TPU:10, one launch (start us, length us, event | category | flops | bytes accessed | tf_op | source)
XLA Modules:
  0.0 178.8 jit_solution(1053716256366969174)
XLA Ops:
  7.2 0.7 all-gather.2.cloned.1.call-update
  7.9 1.3 convert_reduce_fusion
  9.3 0.1 select_reduce_fusion.3
  9.4 1.3 convert_reduce_fusion.2
  10.8 0.7 iota_compare_fusion.12
  11.7 0.7 broadcast_subtract_fusion
  12.4 1.3 convolution_bitcast_fusion
  13.6 0.3 convolution_convert_fusion
  15.3 0.8 copy.32
  16.0 0.8 copy.36
  16.8 1.0 copy.31
  18.8 0.1 select_reduce_fusion.1
  18.9 68.6 %all_gather.7 = bf16[1024,152]{1,0:T(8,128)(2,1)S(1)} all-gather(bf16[32,152]{1,0:T(8,128)(2,1)S(1)} %bitcast.19), channel_id=1, replica_groups=mesh['leaf'=4,'oct'=8] {'leaf','oct'}, dimensions={0}, use_global_device_ids=true | all-gather | bytes 321024 | tf_op jit(solution)/shard_map/all_gather | solution.py:246
  87.5 0.3 fusion.3
  87.8 0.7 abs_reduce_fusion
  89.3 0.1 round-nearest-even_convert_fusion
  89.5 0.1 reshape.141
  89.6 0.2 fusion.15
  89.8 0.7 add.165.tc_ref
  90.5 0.6 pad_bitcast_fusion
  91.1 19.7 %prepare.1 = (bf16[19,152,3072]{2,1,0:T(8,128)(2,1)}, s32[176,384]{1,0:T(8,128)}) custom-call(bf16[152,152,316]{2,1,0:T(8,128)(2,1)} %m_ref.1, s32[144,316]{1,0:T(8,128)} %lf_ref.1, s32[32,316]{1,0:T(8,128)} %lc_ref.1, s32[1,128]{1,0:T(1,128)} %get-tuple-element.23.sf_ref, s32[1,128]{1,0:T(1,128)} %get-tuple-element.22.sc_ref), custom_call_target="tpu_custom_call" | custom-call | bytes 35487744 | tf_op jit(solution)/shard_map/prepare/pallas_call | solution.py:76
  110.8 0.2 select_reduce_fusion
  111.0 3.6 %fusion.2 = f32[152,496]{1,0:T(8,128)S(1)} fusion(bf16[4608,152]{1,0:T(8,128)(2,1)} %all-gather.2.cloned.1.call-done, s32[496]{0:T(512)S(1)} %broadcast_add_fusion), kind=kOutput, calls=%fused_computation.3 | convolution fusion | flops 697098240 | bytes 1704384 | tf_op jit(solution)/shard_map/dot_general | solution.py:198
  114.6 0.8 fusion.10
  116.1 0.2 concatenate.14
  116.4 0.2 fusion.9
  116.6 0.7 add.153.tf_ref
  117.4 51.2 %translate.1 = f32[152,176]{1,0:T(8,128)} custom-call(s32[1]{0:T(128)} %bitcast.pick_ref, s32[176,384]{1,0:T(8,128)} %get-tuple-element.4.idx_ref, s32[19,4,640]{2,1,0:T(4,128)} %add.153.tf_ref, s32[19,4,384]{2,1,0:T(4,128)} %add.165.tc_ref, bf16[19,152,3072]{2,1,0:T(8,128)(2,1)} %get-tuple-element.5.m_ref), custom_call_target="tpu_custom_call" | custom-call | flops 3122921472 | bytes 17743872 | tf_op jit(solution)/shard_map/translate/pallas_call | solution.py:155
  168.6 1.0 slice_multiply_fusion.2
  169.6 0.7 copy.41
  170.2 0.9 slice_multiply_fusion.1
  171.2 0.8 copy.40
  (30 shorter events, 1.3 us)
Async XLA Ops:
  7.2 5.2 %copy-start = (bf16[152,8,152]{2,1,0:T(8,128)(2,1)S(1)}, bf16[152,8,152]{2,1,0:T(8,128)(2,1)}, u32[]{:S(2)}) copy-start(bf16[152,8,152]{2,1,0:T(8,128)(2,1)} %param.12) | copy-start | bytes 1108996
  7.2 103.8 %all-gather.2.cloned.1.call-start = ((), (), s32[]{:S(2)}) async-start(), calls=%async_computation | async-start | bytes 2433024 | tf_op jit(solution)/shard_map/all_gather | solution.py:219
Sparse Core Ops, SparseCore 0:
  10.9 58.1 all-gather.1
